TPU v7x, 128 devices: a whole 4x4x4 slice. The times are simulated.
128 devices in a mesh: feat: 8 (over y, core), ex: 16 (over z, x).
Axes of the slice: x: 4, y: 4, z: 4, core: 2. Of those that a mesh axis runs over, the one named last changes fastest.
Arguments:
- gradients: bfloat16 [16, 67108864], P('ex', 'feat'), may hold values from -6 to 6
- sign_words: int32 [4194304], P('feat'), may hold values from 0 to 65535
- sub_index: int32 [8192], replicated, may hold values from 0 to 67108863, as said below
- test_sketch: bfloat16 [1024, 8192], P('ex'), may hold values from -6 to 6
Outputs:
- scores: float32 [16, 1024], P('ex')
Inputs may be any that keep to these rules, and one draw needn't show every extreme that they name: `sub_index`: strictly increasing; entry k lies in [k * 8192, (k + 1) * 8192); the first entry is 0 and the last is 67108863.
All inputs are finite; a program needn't handle non-finite values.
Results may differ from a plain program's by a relative error of at most 0.0051.
Values may be sent and summed in bfloat16 or wider, within the bound.
A program may use at most 640 MiB of HBM per device.

v0:
```python
import jax
import jax.numpy as jnp
from jax import lax
from jax.sharding import PartitionSpec as P

NHIGH = 1024
NMID = 256
NLOW = 256
K = 8192


def parity_sign(left, right, nbits):
    common = jnp.bitwise_and(left, right)
    total = jnp.zeros_like(common)
    for position in range(nbits):
        total = total + jnp.bitwise_and(jnp.right_shift(common, position), 1)
    return (1 - 2 * (total % 2)).astype(jnp.float32)


def hadamard_table(order):
    places = jnp.arange(order, dtype=jnp.int32)
    return parity_sign(places[:, None], places[None, :], order.bit_length() - 1)


def on_device(gradients, sign_words, sub_index, test_sketch):
    ex_rows = gradients.shape[0]
    local_features = gradients.shape[1]
    feat_place = lax.axis_index("feat")
    high_dev = local_features // (NMID * NLOW)
    all_rows = ex_rows * high_dev
    feature_scale = float(NHIGH * NMID * NLOW) ** (-0.5)
    score_scale = float(K) ** (-0.5)
    lane_rows = local_features // 128
    word_rows = jnp.repeat(sign_words.reshape(lane_rows, 8), 16, axis=1)
    lane_bits = jnp.arange(128, dtype=jnp.int32) % 16
    flags = jnp.bitwise_and(jnp.right_shift(word_rows, lane_bits[None, :]), 1)
    signs = (2 * flags - 1).astype(jnp.bfloat16)
    signed = (gradients.reshape(ex_rows, lane_rows, 128) * signs[None, :, :]).reshape(
        all_rows, NMID, NLOW
    )
    low_table = hadamard_table(NLOW).astype(jnp.bfloat16)
    mid_table = hadamard_table(NMID).astype(jnp.bfloat16)
    first = jnp.einsum("rml,pl->rmp", signed, low_table, preferred_element_type=jnp.float32).astype(
        jnp.bfloat16
    )
    second = jnp.einsum("qm,rmp->rqp", mid_table, first, preferred_element_type=jnp.float32).astype(
        jnp.bfloat16
    )
    second = second.reshape(ex_rows, high_dev, NMID * NLOW)
    high_of = sub_index // (NMID * NLOW)
    col_of = sub_index % (NMID * NLOW)
    high_bits = NHIGH.bit_length() - 1
    rows = feat_place * high_dev + jnp.arange(high_dev, dtype=jnp.int32)
    select = parity_sign(rows[:, None], high_of[None, :], high_bits).astype(jnp.bfloat16)
    picked = jnp.take(second, col_of, axis=2)
    partial_sketch = jnp.einsum("ehk,hk->ek", picked, select, preferred_element_type=jnp.float32)
    sketch = lax.psum(partial_sketch, "feat") * feature_scale
    sketch_rounded = sketch.astype(jnp.bfloat16)
    return (
        jnp.einsum(
            "ek,tk->et",
            sketch_rounded,
            lax.all_gather(test_sketch, "ex", axis=0, tiled=True),
            preferred_element_type=jnp.float32,
        )
        * score_scale
    )


def solution(mesh):
    return jax.shard_map(
        on_device,
        mesh=mesh,
        in_specs=(P("ex", "feat"), P("feat"), P(), P("ex", None)),
        out_specs=P("ex", None),
        check_vma=False,
    )
```

profile of v0, /device:TPU:1, one launch (start us, length us, event | category | flops | bytes accessed | tf_op | source)
XLA Modules:
  0.0 843.6 jit_solution(18058066139032176688)
XLA Ops:
  6.5 0.0 all-gather.2.cloned.1.call-start
  6.5 0.7 all-gather.2.cloned.1.call-update
  7.3 22.1 %reshape.66 = s32[65536,8]{1,0:T(8,128)} reshape(s32[524288]{0:T(1024)} %param.5) | data formatting | bytes 4194304 | tf_op jit(solution)/shard_map/reshape | solution.py:34
  29.4 116.3 %broadcast_in_dim.24 = s32[65536,8,16]{2,1,0:T(8,128)} broadcast(s32[65536,8]{1,0:T(8,128)} %reshape.66), dimensions={0,1} | broadcast | bytes 35651584 | tf_op jit(solution)/shard_map/broadcast_in_dim | solution.py:34
  145.7 179.0 %reshape.67 = s32[128,256,256]{2,1,0:T(8,128)} reshape(s32[65536,8,16]{2,1,0:T(8,128)} %broadcast_in_dim.24) | data formatting | bytes 67108864 | tf_op jit(solution)/shard_map/reshape | solution.py:34
  324.6 354.8 %reduce.1 = bf16[8388608]{0:T(1024)(128)(2,1)} reduce(bf16[1,8388608]{1,0:T(2,128)(2,1)} %param.4, bf16[]{:T(256)} %constant.121), dimensions={0}, to_apply=%param.4.reduce_sub_computation | reduce | bytes 33554432 | tf_op args[0]
  679.5 24.5 %reshape.65 = bf16[128,256,256]{2,1,0:T(8,128)(2,1)} reshape(bf16[8388608]{0:T(1024)(128)(2,1)} %reduce.1) | data formatting | bytes 33554432 | tf_op jit(solution)/shard_map/reshape | solution.py:38
  704.0 26.7 %convert_bitcast_fusion = bf16[128,256,256]{1,2,0:T(8,128)(2,1)} fusion(bf16[128,256,256]{2,1,0:T(8,128)(2,1)} %reshape.65, s32[128,256,256]{2,1,0:T(8,128)} %reshape.67, s32[256]{0:T(256)S(1)} %broadcast_bitcast_fusion), kind=kOutput, calls=%fused_computation.14 | convolution fusion | flops 8687321088 | bytes 67109888 | tf_op jit(solution)/shard_map/qm,rmp->rqp/dot_general | solution.py:46
  730.6 0.0 copy-start
  730.6 24.3 %copy.5 = bf16[128,256,256]{0,2,1:T(8,128)(2,1)} copy(bf16[128,256,256]{1,2,0:T(8,128)(2,1)} %convert_bitcast_fusion) | data formatting | bytes 33554432 | tf_op jit(solution)/shard_map/convert_element_type | solution.py:46
  755.0 0.0 copy-done
  755.0 7.1 fusion.42
  762.2 5.6 copy.11
  767.7 29.8 %gather_fusion = bf16[8192,128]{1,0:T(8,128)(2,1)S(1)} fusion(bf16[128,65536]{0,1:T(8,128)(2,1)} %bitcast.23, s32[8192]{0:T(1024)S(1)} %get-tuple-element.5), kind=kCustom, calls=%fused_computation | custom fusion | bytes 4227072 | tf_op jit(solution)/shard_map/jit(_take)/gather | solution.py:55
  797.6 4.4 multiply_reduce_fusion
  802.1 23.9 %psum.7 = f32[1,8192]{1,0:T(1,128)S(1)} all-reduce(f32[1,8192]{1,0:T(1,128)S(1)} %bitcast.24), channel_id=1, replica_groups=mesh['feat'=8,'ex'=16] {'feat'}, use_global_device_ids=true, to_apply=%region_0.1 | all-reduce | flops 8192 | bytes 65536 | tf_op jit(solution)/shard_map/psum | solution.py:57
  826.0 0.0 all-gather.2.cloned.1.call-done
  826.0 10.2 %fusion.67 = f32[1,1024]{1,0:T(1,128)S(1)} fusion(bf16[1024,8192]{1,0:T(8,128)(2,1)} %all-gather.2.cloned.1.call-done, f32[1,8192]{1,0:T(1,128)S(1)} %psum.7), kind=kOutput, calls=%fused_computation.74 | convolution fusion | flops 16793600 | bytes 16814080 | tf_op jit(solution)/shard_map/ek,tk->et/dot_general | solution.py:60
  836.1 0.6 broadcast_multiply_fusion
  (5 shorter events, 0.1 us)
Async XLA Ops:
  6.5 819.4 %all-gather.2.cloned.1.call-start = ((), (), s32[]{:S(2)}) async-start(), calls=%async_computation | async-start | bytes 17825792 | tf_op jit(solution)/shard_map/all_gather | solution.py:63
  730.6 24.3 %copy-start = (s32[8192]{0:T(1024)S(1)}, s32[8192]{0:T(1024)}, u32[]{:S(2)}) copy-start(s32[8192]{0:T(1024)} %param.6) | copy-start | bytes 98308
Sparse Core Ops, SparseCore 0:
  9.5 114.6 all-gather.1
where the time goes:
time: 850 us; the launch traced here: 844 us
  local copies, waits for them, and re-layouts  402 us (47%)
  other arithmetic  367 us (43%)
  matrix products  36.9 us (4%)
  blocking collectives  23.9 us (3%)
  between operations  13.4 us (2%)
    unnamed x2, other arithmetic  362 us
    reshape x2, local copies, waits for them, and re-layouts, on_device(): word_rows = jnp.repeat(sign_words.reshape(lane_rows, 8), 16, axis=1)  201 us
    broadcast_in_dim x1, local copies, waits for them, and re-layouts, on_device(): word_rows = jnp.repeat(sign_words.reshape(lane_rows, 8), 16, axis=1)  116 us
    gather x1, local copies, waits for them, and re-layouts, on_device(): picked = jnp.take(second, col_of, axis=2)  29.8 us
    dot_general x1, matrix products, on_device(): jnp.einsum('qm,rmp->rqp', mid_table, first, preferred_element_type=jnp.fl...  26.7 us
    reshape x1, local copies, waits for them, and re-layouts, on_device(): gradients.reshape(ex_rows, lane_rows, 128) * signs[None, :, :]  24.5 us
    convert_element_type x1, local copies, waits for them, and re-layouts, on_device(): jnp.einsum('qm,rmp->rqp', mid_table, first, preferred_element_type=jnp.fl...  24.3 us
    psum x1, blocking collectives, on_device(): sketch = lax.psum(partial_sketch, 'feat') * feature_scale  23.9 us
  transfers between devices with their start and end apart: 1, of which 0 were waited for; matrix products, arithmetic and copies ran while one was open for 94% of the time, Pallas kernels for 0%

commit v1 on v0

v1 whole, which is shorter than its diff:
```python
import jax, jax.numpy as jnp, numpy as np
from jax import lax
from jax.experimental import pallas as pl
from jax.experimental.pallas import tpu as pltpu
from jax.sharding import PartitionSpec as P

def hada(n):
    h=np.ones((1,1))
    while h.shape[0]<n: h=np.block([[h,h],[h,-h]])
    return h

def k1_matrix():
    h32, h8 = hada(32), hada(8)
    rows = np.zeros((256,256))
    for j in range(16):
        for t in range(16):
            h5 = j + 16*(t//8); s = t%8
            rows[:, 16*j+t] = np.kron(h32[:,h5], h8[:,s])
    return rows

FB = 16384
NBLK = 16
NS = 6
UPB = FB//2048

def kernel(g_ref, w_ref, km_ref, kp_ref, kq_ref, ks_ref, h4_ref, hm_ref, hb_ref, out_ref,
           raw, words, psel, sq, xs, ts, sem):
    def copies(b, slot):
        h2 = b // 4
        mb = b % 4
        return (pltpu.make_async_copy(g_ref.at[:, h2, :, pl.ds(mb*FB, FB)], raw.at[slot], sem.at[0, slot]),
                pltpu.make_async_copy(w_ref.at[:, h2, pl.ds(mb*8, 8), :], words.at[slot], sem.at[1, slot]))
    for b in range(NS):
        for c in copies(b, b): c.start()
    rows = lax.broadcasted_iota(jnp.int32, (256,256), 0)
    urow = lax.broadcasted_iota(jnp.int32, (32,256), 0)
    @pl.loop(0, 32)
    def _(t):
        onehot = jnp.where(rows == kp_ref[t], 1.0, 0.0).astype(jnp.bfloat16)
        psel[t] = jnp.dot(hb_ref[...], onehot, preferred_element_type=jnp.float32).astype(jnp.bfloat16)
        v = urow & kq_ref[t]
        v = v ^ (v >> 4)
        v = v ^ (v >> 2)
        v = v ^ (v >> 1)
        sq[t] = jnp.where((v & 1) == 1, -1.0, 1.0)
    lane = lax.broadcasted_iota(jnp.int32, (8,128), 1)
    sub = lax.broadcasted_iota(jnp.int32, (8,128), 0)
    base = sub*8 + lane//16
    bit_lo = jnp.left_shift(1, lane % 16)
    bit_hi = jnp.left_shift(1, lane % 16 + 16)

    @pl.loop(0, NBLK)
    def _(b):
        slot = b % NS
        for c in copies(b, slot): c.wait()
        @pl.loop(0, UPB//2)
        def _(pair):
            outs = []
            for uu in range(2):
                u = pair*2 + uu
                for j in range(16):
                    wlo = words[slot, j, pl.ds(u, 1), :]
                    whi = words[slot, j+16, pl.ds(u, 1), :]
                    wp = jnp.broadcast_to(wlo | (whi << 16), (8,128))
                    for gam in range(2):
                        y = jnp.take_along_axis(wp, base + gam*64, axis=1)
                        parts = []
                        for hh, bit in ((j, bit_lo), (j+16, bit_hi)):
                            x = raw[slot, hh, :, pl.ds(pl.multiple_of(u*2048 + gam*1024, 1024), 1024)]
                            x = x.astype(jnp.float32).reshape(8,128)
                            parts.append(jnp.where((y & bit) != 0, x, -x))
                        xs[uu, 16*j:16*j+16, gam*128:gam*128+128] = jnp.concatenate(parts, axis=0).astype(jnp.bfloat16)
            for uu in range(2):
                outs.append(jnp.dot(hm_ref[...], xs[uu], preferred_element_type=jnp.float32))
            r0 = pl.multiple_of(b*(UPB*8) + pair*16, 16)
            for t in range(32):
                ts[t, pl.ds(r0, 16), :] = jnp.concatenate([outs[0][8*t:8*t+8], outs[1][8*t:8*t+8]], axis=0).astype(jnp.bfloat16)
        @pl.when(b + NS < NBLK)
        def _():
            for c in copies(b + NS, slot): c.start()

    sub256 = lax.broadcasted_iota(jnp.int32, (8,256), 0)
    @pl.loop(0, 32)
    def _(t):
        u = jnp.dot(ts[t], psel[t], preferred_element_type=jnp.float32)
        total = jnp.zeros((8,256), jnp.float32)
        accs = [jnp.zeros((8,256), jnp.float32) for _ in range(4)]
        for m in range(32):
            s = jnp.broadcast_to(sq[t, m:m+1, :], (8,256))
            for h2 in range(4):
                accs[h2] = accs[h2] + u[h2*256+m*8:h2*256+m*8+8] * s
        for h2 in range(4):
            total = total + accs[h2] * h4_ref[h2:h2+1, :]
        total = jnp.where(sub256 == ks_ref[t], total, 0.0)
        out_ref[pl.ds(t,1), :] = jnp.sum(total, axis=0, keepdims=True)

def sketch_partial(gradients, sign_words, sub_index):
    g = gradients.reshape(32, 4, 1, 65536)
    w = sign_words.reshape(32, 4, 32, 128)
    c = sub_index.reshape(8, 32, 32).transpose(1,0,2).reshape(32,1,256) & 65535
    kp = ((c >> 10) & 1)*128 + (c & 127)
    kq = c >> 11
    ks = (c >> 7) & 7
    col = np.arange(256)
    hh2 = (col >> 3) & 3
    h4 = jnp.asarray(hada(4)[:, hh2], jnp.float32)
    hm = jnp.asarray(k1_matrix(), jnp.bfloat16)
    hb = jnp.asarray(hada(256), jnp.bfloat16)
    anyspec = pl.BlockSpec(memory_space=pl.ANY)
    vm = pl.BlockSpec(memory_space=pltpu.VMEM)
    return pl.pallas_call(
        kernel,
        out_shape=jax.ShapeDtypeStruct((32,256), jnp.float32),
        in_specs=[anyspec, anyspec, vm, vm, vm, vm, vm, vm, vm],
        out_specs=vm,
        scratch_shapes=[
            pltpu.VMEM((NS, 32, 1, FB), jnp.bfloat16),
            pltpu.VMEM((NS, 32, 8, 128), jnp.int32),
            pltpu.VMEM((32, 256, 256), jnp.bfloat16),
            pltpu.VMEM((32, 32, 256), jnp.float32),
            pltpu.VMEM((2, 256, 256), jnp.bfloat16),
            pltpu.VMEM((32, 1024, 256), jnp.bfloat16),
            pltpu.SemaphoreType.DMA((2, NS)),
        ],
        compiler_params=pltpu.CompilerParams(vmem_limit_bytes=60*1024*1024),
    )(g, w, c, kp, kq, ks, h4, hm, hb)

def on_device(gradients, sign_words, sub_index, test_sketch):
    feat = lax.axis_index("feat")
    part = sketch_partial(gradients, sign_words, sub_index)
    g3 = np.arange(256) >> 5
    sgn = jnp.asarray(hada(8)[:, g3], jnp.float32)[feat]
    part = (part * sgn[None, :]).reshape(32, 8, 32).transpose(1,0,2).reshape(1, 8192)
    sketch = lax.psum(part, "feat") * (float(67108864) ** -0.5)
    sk = sketch.astype(jnp.bfloat16)
    allsk = lax.all_gather(sk, "ex", axis=0, tiled=True)
    sc = jnp.einsum("ek,tk->et", allsk, test_sketch, preferred_element_type=jnp.float32)
    sc = sc * (8192.0 ** -0.5)
    out = lax.all_to_all(sc.reshape(16,1,64), "ex", split_axis=0, concat_axis=1, tiled=True)
    return out.reshape(1, 1024)

def solution(mesh):
    return jax.shard_map(on_device, mesh=mesh,
        in_specs=(P("ex", "feat"), P("feat"), P(), P("ex", None)),
        out_specs=P("ex", None), check_vma=False)
```

time: 850 us -> 117 us (0.14)
  the two profiles are of different devices: /device:TPU:1 before, /device:TPU:0 now
where the time goes in v1:
time: 117 us; the launch traced here: 116 us
  blocking collectives  63.6 us (54%)
  Pallas kernels  46.7 us (40%)
  other arithmetic  3.03 us (3%)
  local copies, waits for them, and re-layouts  2.39 us (2%)
    pallas_call x1, Pallas kernels, sketch_partial(): pl.pallas_call(kernel, out_shape=jax.ShapeDtypeStruct((32, 256), jnp.floa...  46.7 us
    psum x1, blocking collectives, on_device(): sketch = lax.psum(part, 'feat') * float(67108864) ** (-0.5)  26 us
    all_gather x1, blocking collectives, on_device(): allsk = lax.all_gather(sk, 'ex', axis=0, tiled=True)  25.4 us
    all_to_all x1, blocking collectives, on_device(): lax.all_to_all(sc.reshape(16, 1, 64), 'ex', split_axis=0, concat_axis=1,...  12.3 us

profile of v1, /device:TPU:0, one launch (start us, length us, event | category | flops | bytes accessed | tf_op | source)
XLA Modules:
  0.0 116.4 jit_solution(121976646105985131)
XLA Ops:
  0.0 0.0 copy-start
  0.0 0.8 broadcast_and_fusion
  0.9 0.1 and.46
  0.9 0.1 copy.14
  1.0 0.1 and.48.km_ref
  1.2 0.0 copy-start.1
  1.2 0.7 shift-right-arithmetic_and_fusion
  1.9 0.7 constant_dynamic-slice_fusion
  2.6 0.0 copy-done.1
  2.6 46.7 %shard_map.82 = f32[32,256]{1,0:T(8,128)} custom-call(bf16[32,4,1,65536]{3,2,1,0:T(2,128)(2,1)} %bitcast.16, s32[32,4,32,128]{3,2,1,0:T(8,128)} %bitcast.17, s32[32,1,256]{2,1,0:T(1,128)} %copy-done.1, s32[32,1,256]{2,1,0:T(1,128)} %get-tuple-element.7.kp_ref, s32[32,1,256]{2,1,0:T(1,128)} %get-tuple-element.6.kq_ref, ...), custom_call_target="tpu_custom_call" | custom-call | tf_op jit(solution)/shard_map/pallas_call | solution.py:111
  49.3 0.8 broadcast_multiply_fusion
  50.1 0.1 reshape.86
  50.2 0.1 reshape.87
  50.3 26.0 %psum.7 = f32[1,8192]{1,0:T(1,128)S(1)} all-reduce(f32[1,8192]{1,0:T(1,128)S(1)} %reshape.87), channel_id=1, replica_groups=mesh['feat'=8,'ex'=16] {'feat'}, use_global_device_ids=true, to_apply=%region_0.0 | all-reduce | flops 8192 | bytes 65536 | tf_op jit(solution)/shard_map/psum | solution.py:134
  76.3 25.4 %all-gather = bf16[16,1,8192]{2,1,0:T(2,128)(2,1)S(1)} all-gather(bf16[1,1,8192]{2,1,0:T(2,128)(2,1)S(1)} %convert_bitcast_fusion), channel_id=1, replica_groups=mesh['feat'=8,'ex'=16] {'ex'}, dimensions={0}, use_global_device_ids=true | all-gather | bytes 278528 | tf_op jit(solution)/shard_map/all_gather | solution.py:136
  101.7 0.0 copy-done
  101.7 0.5 convolution_multiply_fusion
  102.2 12.3 %all_to_all.4 = f32[16,1,64]{2,1,0:T(1,128)S(1)} all-to-all(f32[16,1,64]{2,1,0:T(1,128)S(1)} %bitcast.20), channel_id=1, replica_groups=mesh['feat'=8,'ex'=16] {'ex'}, dimensions={0} | all-to-all | bytes 8192 | tf_op jit(solution)/shard_map/all_to_all | solution.py:139
  114.5 0.5 broadcast.90
  115.0 0.7 reduce.3
  115.7 0.7 reshape.89
  (2 shorter events, 0.1 us)
Async XLA Ops:
  0.0 101.7 %copy-start = (bf16[64,8192]{1,0:T(8,128)(2,1)S(1)}, bf16[64,8192]{1,0:T(8,128)(2,1)}, u32[]{:S(2)}) copy-start(bf16[64,8192]{1,0:T(8,128)(2,1)} %param.11) | copy-start | bytes 3145732
  1.2 1.4 %copy-start.1 = (s32[32,1,256]{2,1,0:T(1,128)}, s32[32,1,256]{2,1,0:T(1,128)S(1)}, u32[]{:S(2)}) copy-start(s32[32,1,256]{2,1,0:T(1,128)S(1)} %and.48.km_ref) | copy-start | bytes 98308

commit v2 on v1

--- a/solution.py
+++ b/solution.py
@@ -80,19 +80,28 @@
             for c in copies(b + NS, slot): c.start()
 
     sub256 = lax.broadcasted_iota(jnp.int32, (8,256), 0)
-    @pl.loop(0, 32)
-    def _(t):
-        u = jnp.dot(ts[t], psel[t], preferred_element_type=jnp.float32)
-        total = jnp.zeros((8,256), jnp.float32)
-        accs = [jnp.zeros((8,256), jnp.float32) for _ in range(4)]
-        for m in range(32):
-            s = jnp.broadcast_to(sq[t, m:m+1, :], (8,256))
+    spread = (sub % 4)*32 + lane % 32
+    @pl.loop(0, 8)
+    def _(part):
+        chunk = jnp.zeros((8,128), jnp.float32)
+        for a in range(4):
+            t = part*4 + a
+            u = jnp.dot(ts[t], psel[t], preferred_element_type=jnp.float32)
+            accs = [jnp.zeros((8,256), jnp.float32) for _ in range(4)]
+            for m in range(32):
+                s = jnp.broadcast_to(sq[t, m:m+1, :], (8,256))
+                for h2 in range(4):
+                    accs[h2] = accs[h2] + u[h2*256+m*8:h2*256+m*8+8] * s
+            total = jnp.zeros((8,256), jnp.float32)
             for h2 in range(4):
-                accs[h2] = accs[h2] + u[h2*256+m*8:h2*256+m*8+8] * s
-        for h2 in range(4):
-            total = total + accs[h2] * h4_ref[h2:h2+1, :]
-        total = jnp.where(sub256 == ks_ref[t], total, 0.0)
-        out_ref[pl.ds(t,1), :] = jnp.sum(total, axis=0, keepdims=True)
+                total = total + accs[h2] * h4_ref[h2:h2+1, :]
+            total = jnp.where(sub256 == ks_ref[t], total, 0.0)
+            row = jnp.broadcast_to(jnp.sum(total, axis=0, keepdims=True), (8,256))
+            row = jnp.where(sub < 4, row[:, :128], row[:, 128:])
+            row = jnp.take_along_axis(row, spread, axis=1)
+            chunk = jnp.where(lane // 32 == a, row, chunk)
+        for g in range(8):
+            out_ref[g, pl.ds(part, 1), :] = chunk[g:g+1]
 
 def sketch_partial(gradients, sign_words, sub_index):
     g = gradients.reshape(32, 4, 1, 65536)
@@ -110,7 +119,7 @@
     vm = pl.BlockSpec(memory_space=pltpu.VMEM)
     return pl.pallas_call(
         kernel,
-        out_shape=jax.ShapeDtypeStruct((32,256), jnp.float32),
+        out_shape=jax.ShapeDtypeStruct((8,8,128), jnp.float32),
         in_specs=[anyspec, anyspec, vm, vm, vm, vm, vm, vm, vm],
         out_specs=vm,
         scratch_shapes=[
@@ -123,21 +132,83 @@
             pltpu.SemaphoreType.DMA((2, NS)),
         ],
         compiler_params=pltpu.CompilerParams(vmem_limit_bytes=60*1024*1024),
+        cost_estimate=pl.CostEstimate(flops=17_000_000_000, bytes_accessed=36*1024*1024, transcendentals=0),
     )(g, w, c, kp, kq, ks, h4, hm, hb)
+
+FEATS = 8
+MESH = pl.DeviceIdType.MESH
+
+def tail_kernel(part_ref, tests_ref, out_ref, tests, recv1, recv2, mine, send1, got1, send2, got2, tsem):
+    me = lax.axis_index("feat")
+    tcopy = pltpu.make_async_copy(tests_ref, tests, tsem)
+    tcopy.start()
+    barrier = pltpu.get_barrier_semaphore()
+    peers = [lax.rem(me + d, FEATS) for d in range(1, FEATS)]
+    for p in peers:
+        pl.semaphore_signal(barrier, inc=1, device_id={"feat": p}, device_id_type=MESH)
+    pl.semaphore_wait(barrier, FEATS - 1)
+    def first(src, slot, p, d):
+        return pltpu.make_async_remote_copy(src_ref=part_ref.at[src], dst_ref=recv1.at[slot], send_sem=send1.at[d],
+            recv_sem=got1.at[slot], device_id={"feat": p}, device_id_type=MESH)
+    for d, p in enumerate(peers):
+        first(p, me, p, d).start()
+    recv1[me] = part_ref[me]
+    for d, p in enumerate(peers):
+        first(p, p, p, d).wait_recv()
+    sk = recv1[0]
+    for f in range(1, FEATS):
+        common = me & f
+        parity = (common ^ (common >> 1) ^ (common >> 2)) & 1
+        sk = sk + recv1[f] * (1 - 2*parity).astype(jnp.float32)
+    sk = sk * (float(67108864) ** -0.5)
+    row = jnp.concatenate([sk[g:g+1] for g in range(8)], axis=1)
+    lhs = jnp.broadcast_to(row, (16, 1024)).astype(jnp.bfloat16)
+    tcopy.wait()
+    res = lax.dot_general(lhs, tests[...], (((1,), (1,)), ((), ())), preferred_element_type=jnp.float32)
+    mine[...] = res[0:1]
+    def second(slot, p, d):
+        return pltpu.make_async_remote_copy(src_ref=mine, dst_ref=recv2.at[slot], send_sem=send2.at[d],
+            recv_sem=got2.at[slot], device_id={"feat": p}, device_id_type=MESH)
+    for d, p in enumerate(peers):
+        second(me, p, d).start()
+    recv2[me] = res[0:1]
+    for d, p in enumerate(peers):
+        second(p, p, d).wait_recv()
+    total = recv2[0]
+    for f in range(1, FEATS):
+        total = total + recv2[f]
+    out_ref[...] = total * (8192.0 ** -0.5)
+    for d, p in enumerate(peers):
+        first(p, me, p, d).wait_send()
+        second(me, p, d).wait_send()
+
+def scores_of(part, tests):
+    vm = pl.BlockSpec(memory_space=pltpu.VMEM)
+    return pl.pallas_call(
+        tail_kernel,
+        out_shape=jax.ShapeDtypeStruct((1,1024), jnp.float32),
+        in_specs=[vm, pl.BlockSpec(memory_space=pl.ANY)],
+        out_specs=vm,
+        scratch_shapes=[
+            pltpu.VMEM((1024, 1024), jnp.bfloat16),
+            pltpu.VMEM((FEATS, 8, 128), jnp.float32),
+            pltpu.VMEM((FEATS, 1, 1024), jnp.float32),
+            pltpu.VMEM((1, 1024), jnp.float32),
+            pltpu.SemaphoreType.DMA((FEATS - 1,)),
+            pltpu.SemaphoreType.DMA((FEATS,)),
+            pltpu.SemaphoreType.DMA((FEATS - 1,)),
+            pltpu.SemaphoreType.DMA((FEATS,)),
+            pltpu.SemaphoreType.DMA,
+        ],
+        compiler_params=pltpu.CompilerParams(collective_id=0, has_side_effects=True, vmem_limit_bytes=60*1024*1024),
+    )(part, tests)
 
 def on_device(gradients, sign_words, sub_index, test_sketch):
     feat = lax.axis_index("feat")
+    cols = lax.dynamic_slice_in_dim(test_sketch, feat*1024, 1024, axis=1)
+    tests = lax.all_gather(cols, "ex", axis=0, tiled=True)
     part = sketch_partial(gradients, sign_words, sub_index)
-    g3 = np.arange(256) >> 5
-    sgn = jnp.asarray(hada(8)[:, g3], jnp.float32)[feat]
-    part = (part * sgn[None, :]).reshape(32, 8, 32).transpose(1,0,2).reshape(1, 8192)
-    sketch = lax.psum(part, "feat") * (float(67108864) ** -0.5)
-    sk = sketch.astype(jnp.bfloat16)
-    allsk = lax.all_gather(sk, "ex", axis=0, tiled=True)
-    sc = jnp.einsum("ek,tk->et", allsk, test_sketch, preferred_element_type=jnp.float32)
-    sc = sc * (8192.0 ** -0.5)
-    out = lax.all_to_all(sc.reshape(16,1,64), "ex", split_axis=0, concat_axis=1, tiled=True)
-    return out.reshape(1, 1024)
+    return scores_of(part, tests)
 
 def solution(mesh):
     return jax.shard_map(on_device, mesh=mesh,

time: 117 us -> 79.1 us (0.68)
  the two profiles are of different devices: /device:TPU:0 before, /device:TPU:1 now
where the time goes in v2:
time: 79.1 us; the launch traced here: 78.8 us
  Pallas kernels  56.8 us (72%)
  between operations  13.4 us (17%)
  waiting for transfers between devices  3.57 us (5%)
  local copies, waits for them, and re-layouts  3.44 us (4%)
  other arithmetic  1.48 us (2%)
    pallas_call x1, Pallas kernels, sketch_partial(): pl.pallas_call(kernel, out_shape=jax.ShapeDtypeStruct((8, 8, 128), jnp.fl...  43.2 us
    pallas_call x1, Pallas kernels, scores_of(): pl.pallas_call(tail_kernel, out_shape=jax.ShapeDtypeStruct((1, 1024), jnp...  13.7 us
    all_gather x1, waiting for transfers between devices, on_device(): tests = lax.all_gather(cols, 'ex', axis=0, tiled=True)  3.56 us
    unnamed x5, local copies, waits for them, and re-layouts  2.51 us
  transfers between devices with their start and end apart: 1, of which 1 were waited for; matrix products, arithmetic and copies ran while one was open for 2% of the time, Pallas kernels for 55%

profile of v2, /device:TPU:1, one launch (start us, length us, event | category | flops | bytes accessed | tf_op | source)
XLA Modules:
  0.0 78.8 jit_solution(1138171380810723573)
XLA Ops:
  6.5 0.0 copy-start
  6.5 0.0 all-gather.2.cloned.1.call-start
  6.5 1.2 %copy-done = bf16[64,8192]{1,0:T(8,128)(2,1)S(1)} copy-done((bf16[64,8192]{1,0:T(8,128)(2,1)S(1)}, bf16[64,8192]{1,0:T(8,128)(2,1)}, u32[]{:S(2)}) %copy-start) | copy-done | bytes 1048600
  7.8 0.7 constant_dynamic-slice_fusion
  8.4 0.0 all-gather.2.cloned.1.call-update
  8.4 0.8 broadcast_and_fusion
  9.2 0.1 and.46
  9.3 0.1 copy.9
  9.4 0.1 and.48.km_ref
  9.5 0.0 copy-start.1
  9.5 0.7 shift-right-arithmetic_and_fusion
  10.2 0.0 copy-done.1
  10.2 43.2 %shard_map.73.part_ref = f32[8,8,128]{2,1,0:T(8,128)} custom-call(bf16[32,4,1,65536]{3,2,1,0:T(2,128)(2,1)} %bitcast.4, s32[32,4,32,128]{3,2,1,0:T(8,128)} %bitcast.5, s32[32,1,256]{2,1,0:T(1,128)} %copy-done.1, s32[32,1,256]{2,1,0:T(1,128)} %get-tuple-element.7.kp_ref, s32[32,1,256]{2,1,0:T(1,128)} %get-tuple-element.6.kq_ref, ...), custom_call_target="tpu_custom_call" | custom-call | flops 16999999488 | bytes 37748736 | tf_op jit(solution)/shard_map/pallas_call | solution.py:120
  53.4 3.6 %all-gather.2.cloned.1.call-done.tests_ref = bf16[1024,1024]{1,0:T(8,128)(2,1)} async-done(((bf16[64,1024]{1,0:T(8,128)(2,1)}), bf16[1024,1024]{1,0:T(8,128)(2,1)}) %all-gather.2.cloned.1.call-update) | async-done | bytes 2097168 | tf_op jit(solution)/shard_map/all_gather | solution.py:209
  57.0 13.7 %shard_map.74 = f32[1,1024]{1,0:T(1,128)} custom-call(f32[8,8,128]{2,1,0:T(8,128)} %shard_map.73.part_ref, bf16[1024,1024]{1,0:T(8,128)(2,1)} %all-gather.2.cloned.1.call-done.tests_ref), custom_call_target="tpu_custom_call" | custom-call | tf_op jit(solution)/shard_map/pallas_call | solution.py:187
  70.6 1.3 %copy.12 = f32[1,1024]{1,0:T(1,128)} copy(f32[1,1024]{1,0:T(1,128)} %shard_map.74) | data formatting | bytes 8192
Async XLA Ops:
  6.5 1.2 %copy-start = (bf16[64,8192]{1,0:T(8,128)(2,1)S(1)}, bf16[64,8192]{1,0:T(8,128)(2,1)}, u32[]{:S(2)}) copy-start(bf16[64,8192]{1,0:T(8,128)(2,1)} %param.10) | copy-start | bytes 3145732
  6.5 50.4 %all-gather.2.cloned.1.call-start = ((), (), s32[]{:S(2)}) async-start(), calls=%async_computation | async-start | bytes 2228224 | tf_op jit(solution)/shard_map/all_gather | solution.py:209
  9.5 0.7 copy-start.1
Sparse Core Ops, SparseCore 0:
  9.5 47.4 all-gather.1

commit v3 on v2

v3 whole, which is shorter than its diff:
```python
import jax, jax.numpy as jnp, numpy as np
from jax import lax
from jax.experimental import pallas as pl
from jax.experimental.pallas import tpu as pltpu
from jax.sharding import PartitionSpec as P

def hada(n):
    h=np.ones((1,1))
    while h.shape[0]<n: h=np.block([[h,h],[h,-h]])
    return h

def k1_matrix():
    h32, h8 = hada(32), hada(8)
    rows = np.zeros((256,256))
    for j in range(16):
        for t in range(16):
            h5 = j + 16*(t//8); s = t%8
            rows[:, 16*j+t] = np.kron(h32[:,h5], h8[:,s])
    return rows

FB = 8192
NBLK = 32
NS = 12
UNITS = 4
TUNROLL = 4

def kernel(g_ref, w_ref, kp_ref, kq_ref, ks_ref, h4_ref, hm_ref, hb_ref, out_ref,
           raw, words, psel, sq, xs0, xs1, ts, sem, wsem):
    def gcopy(b):
        return pltpu.make_async_copy(g_ref.at[:, b // 8, :, pl.ds(pl.multiple_of((b % 8)*FB, FB), FB)], raw.at[b % NS], sem.at[b % NS])
    def wcopy(h2):
        return pltpu.make_async_copy(w_ref.at[:, h2], words.at[h2], wsem.at[h2])
    wcopy(0).start()
    for b in range(NS):
        gcopy(b).start()
    for h2 in range(1, 4):
        wcopy(h2).start()
    rows = lax.broadcasted_iota(jnp.int32, (256,256), 0)
    urow = lax.broadcasted_iota(jnp.int32, (32,256), 0)
    @pl.loop(0, 32//TUNROLL)
    def _(tt):
        for dt in range(TUNROLL):
            t = tt*TUNROLL + dt
            onehot = jnp.where(rows == kp_ref[t], 1.0, 0.0).astype(jnp.bfloat16)
            psel[t] = jnp.dot(hb_ref[...], onehot, preferred_element_type=jnp.float32).astype(jnp.bfloat16)
            v = urow & kq_ref[t]
            v = v ^ (v >> 4)
            v = v ^ (v >> 2)
            v = v ^ (v >> 1)
            sq[t] = jnp.where((v & 1) == 1, -1.0, 1.0)
    lane = lax.broadcasted_iota(jnp.int32, (8,128), 1)
    sub = lax.broadcasted_iota(jnp.int32, (8,128), 0)
    base = sub*8 + lane//16
    bit_lo = jnp.left_shift(1, lane % 16)
    bit_hi = jnp.left_shift(1, lane % 16 + 16)

    def prep(b, xs):
        slot = b % NS
        h2 = b // 8
        r0 = (b % 8)*UNITS
        for u in range(UNITS):
            for j in range(16):
                wlo = words[h2, j, pl.ds(r0 + u, 1), :]
                whi = words[h2, j+16, pl.ds(r0 + u, 1), :]
                wp = jnp.broadcast_to(wlo | (whi << 16), (8,128))
                for gam in range(2):
                    y = jnp.take_along_axis(wp, base + gam*64, axis=1)
                    parts = []
                    for hh, bit in ((j, bit_lo), (j+16, bit_hi)):
                        x = raw[slot, hh, :, u*2048 + gam*1024:u*2048 + gam*1024+1024]
                        x = x.astype(jnp.float32).reshape(8,128)
                        parts.append(jnp.where((y & bit) != 0, x, -x))
                    xs[16*j:16*j+16, u*256+gam*128:u*256+gam*128+128] = jnp.concatenate(parts, axis=0).astype(jnp.bfloat16)

    def mix(b, xs):
        for pair in range(UNITS//2):
            outs = [jnp.dot(hm_ref[...], xs[:, (2*pair+uu)*256:(2*pair+uu)*256+256], preferred_element_type=jnp.float32) for uu in range(2)]
            r0 = pl.multiple_of(b*(UNITS*8) + pair*16, 16)
            for t in range(32):
                ts[t, pl.ds(r0, 16), :] = jnp.concatenate([outs[0][8*t:8*t+8], outs[1][8*t:8*t+8]], axis=0).astype(jnp.bfloat16)

    def arrive(b):
        @pl.when(b < NBLK)
        def _():
            gcopy(b).wait()
        @pl.when((b < NBLK) & (b % 8 == 0))
        def _():
            wcopy(b // 8).wait()
    def refill(b):
        @pl.when(b < NBLK)
        def _():
            gcopy(b).start()

    arrive(0)
    prep(0, xs0)
    refill(NS)
    @pl.loop(0, NBLK//2)
    def _(i):
        b = 2*i
        arrive(b + 1)
        prep(b + 1, xs1)
        mix(b, xs0)
        refill(b + 1 + NS)
        arrive(b + 2)
        prep(jnp.minimum(b + 2, NBLK - 1), xs0)
        mix(b + 1, xs1)
        refill(b + 2 + NS)

    sub256 = lax.broadcasted_iota(jnp.int32, (8,256), 0)
    spread = (sub % 4)*32 + lane % 32
    @pl.loop(0, 8)
    def _(part):
        chunk = jnp.zeros((8,128), jnp.float32)
        for a in range(4):
            t = part*4 + a
            u = jnp.dot(ts[t], psel[t], preferred_element_type=jnp.float32)
            accs = [jnp.zeros((8,256), jnp.float32) for _ in range(4)]
            for m in range(32):
                s = jnp.broadcast_to(sq[t, m:m+1, :], (8,256))
                for h2 in range(4):
                    accs[h2] = accs[h2] + u[h2*256+m*8:h2*256+m*8+8] * s
            total = jnp.zeros((8,256), jnp.float32)
            for h2 in range(4):
                total = total + accs[h2] * h4_ref[h2:h2+1, :]
            total = jnp.where(sub256 == ks_ref[t], total, 0.0)
            row = jnp.broadcast_to(jnp.sum(total, axis=0, keepdims=True), (8,256))
            row = jnp.where(sub < 4, row[:, :128], row[:, 128:])
            row = jnp.take_along_axis(row, spread, axis=1)
            chunk = jnp.where(lane // 32 == a, row, chunk)
        for g in range(8):
            out_ref[g, pl.ds(part, 1), :] = chunk[g:g+1]

def sketch_partial(gradients, sign_words, sub_index):
    g = gradients.reshape(32, 4, 1, 65536)
    w = sign_words.reshape(32, 4, 32, 128)
    c = sub_index.reshape(8, 32, 32).transpose(1,0,2).reshape(32,1,256) & 65535
    kp = ((c >> 10) & 1)*128 + (c & 127)
    kq = c >> 11
    ks = (c >> 7) & 7
    col = np.arange(256)
    hh2 = (col >> 3) & 3
    h4 = jnp.asarray(hada(4)[:, hh2], jnp.float32)
    hm = jnp.asarray(k1_matrix(), jnp.bfloat16)
    hb = jnp.asarray(hada(256), jnp.bfloat16)
    anyspec = pl.BlockSpec(memory_space=pl.ANY)
    vm = pl.BlockSpec(memory_space=pltpu.VMEM)
    return pl.pallas_call(
        kernel,
        out_shape=jax.ShapeDtypeStruct((8,8,128), jnp.float32),
        in_specs=[anyspec, anyspec, vm, vm, vm, vm, vm, vm],
        out_specs=vm,
        scratch_shapes=[
            pltpu.VMEM((NS, 32, 1, FB), jnp.bfloat16),
            pltpu.VMEM((4, 32, 32, 128), jnp.int32),
            pltpu.VMEM((32, 256, 256), jnp.bfloat16),
            pltpu.VMEM((32, 32, 256), jnp.float32),
            pltpu.VMEM((256, UNITS*256), jnp.bfloat16),
            pltpu.VMEM((256, UNITS*256), jnp.bfloat16),
            pltpu.VMEM((32, 1024, 256), jnp.bfloat16),
            pltpu.SemaphoreType.DMA((NS,)),
            pltpu.SemaphoreType.DMA((4,)),
        ],
        compiler_params=pltpu.CompilerParams(vmem_limit_bytes=60*1024*1024),
        cost_estimate=pl.CostEstimate(flops=17_000_000_000, bytes_accessed=36*1024*1024, transcendentals=0),
    )(g, w, kp, kq, ks, h4, hm, hb)

FEATS, EXS = 8, 16
MESH = pl.DeviceIdType.MESH

def tail_kernel(part_ref, tests_ref, out_ref, tests, recv1, recv2, recv3, recv4, mine1, mine2,
                send1, got1, send2, got2, send3, got3, send4, got4, tsem):
    feat = lax.axis_index("feat")
    ex = lax.axis_index("ex")
    tcopy = pltpu.make_async_copy(tests_ref.at[:, pl.ds(pl.multiple_of(feat*1024, 1024), 1024)], tests, tsem)
    tcopy.start()
    barrier = pltpu.get_barrier_semaphore()
    fpeers = [lax.rem(feat + d, FEATS) for d in range(1, FEATS)]
    epeers = [lax.rem(ex + d, EXS) for d in range(1, EXS)]
    for p in fpeers:
        pl.semaphore_signal(barrier, inc=1, device_id={"feat": p}, device_id_type=MESH)
    for p in epeers:
        pl.semaphore_signal(barrier, inc=1, device_id={"ex": p}, device_id_type=MESH)
    pl.semaphore_wait(barrier, FEATS + EXS - 2)

    def exchange(peers, axis, src_of, dst, send, got):
        me = feat if axis == "feat" else ex
        def copy(slot, p, d):
            return pltpu.make_async_remote_copy(src_ref=src_of(p), dst_ref=dst.at[slot], send_sem=send.at[d],
                recv_sem=got.at[slot], device_id={axis: p}, device_id_type=MESH)
        sent = [copy(me, p, d) for d, p in enumerate(peers)]
        for c in sent:
            c.start()
        return sent, [copy(p, p, d) for d, p in enumerate(peers)]

    waits = []
    sent, come = exchange(fpeers, "feat", lambda p: part_ref.at[p], recv1, send1, got1)
    waits += sent
    recv1[feat] = part_ref[feat]
    for c in come: c.wait_recv()
    sk = jnp.zeros((8,128), jnp.float32)
    for f in range(FEATS):
        common = feat & f
        parity = (common ^ (common >> 1) ^ (common >> 2)) & 1
        sk = sk + recv1[f] * (1 - 2*parity).astype(jnp.float32)
    sk = sk * (float(67108864) ** -0.5)
    sk = sk.astype(jnp.bfloat16).astype(jnp.float32)
    mine1[...] = sk
    sent, come = exchange(epeers, "ex", lambda p: mine1, recv2, send2, got2)
    waits += sent
    recv2[ex] = sk
    tcopy.wait()
    for c in come: c.wait_recv()
    res = jnp.zeros((EXS, 64), jnp.float32)
    for g in range(8):
        lhs = recv2[:, g, :].astype(jnp.bfloat16)
        res = res + lax.dot_general(lhs, tests[:, g*128:g*128+128], (((1,), (1,)), ((), ())), preferred_element_type=jnp.float32)
    wide = jnp.concatenate([res, res], axis=1)
    half = lax.broadcasted_iota(jnp.int32, (EXS, 128), 1) // 64
    wide = jnp.where(half == lax.rem(ex, 2), wide, 0.0)
    for e in range(EXS):
        mine2[e] = wide[e:e+1]
    sent, come = exchange(epeers, "ex", lambda p: mine2.at[p], recv3, send3, got3)
    waits += sent
    recv3[ex] = mine2[ex]
    for c in come: c.wait_recv()
    for j in range(8):
        mine1b = recv3[2*j] + recv3[2*j+1]
        recv4[feat, pl.ds(j, 1), :] = mine1b
    sent, come = exchange(fpeers, "feat", lambda p: recv4.at[feat], recv4, send4, got4)
    waits += sent
    for c in come: c.wait_recv()
    total = recv4[0]
    for f in range(1, FEATS):
        total = total + recv4[f]
    out_ref[...] = total
    for c in waits:
        c.wait_send()

def scores_of(part, tests):
    vm = pl.BlockSpec(memory_space=pltpu.VMEM)
    dma = pltpu.SemaphoreType.DMA
    return pl.pallas_call(
        tail_kernel,
        out_shape=jax.ShapeDtypeStruct((8,128), jnp.float32),
        in_specs=[vm, pl.BlockSpec(memory_space=pl.ANY)],
        out_specs=vm,
        scratch_shapes=[
            pltpu.VMEM((64, 1024), jnp.bfloat16),
            pltpu.VMEM((FEATS, 8, 128), jnp.float32),
            pltpu.VMEM((EXS, 8, 128), jnp.float32),
            pltpu.VMEM((EXS, 1, 128), jnp.float32),
            pltpu.VMEM((FEATS, 8, 128), jnp.float32),
            pltpu.VMEM((8, 128), jnp.float32),
            pltpu.VMEM((EXS, 1, 128), jnp.float32),
            dma((FEATS - 1,)), dma((FEATS,)), dma((EXS - 1,)), dma((EXS,)),
            dma((EXS - 1,)), dma((EXS,)), dma((FEATS - 1,)), dma((FEATS,)), dma,
        ],
        compiler_params=pltpu.CompilerParams(collective_id=0, has_side_effects=True, vmem_limit_bytes=60*1024*1024),
    )(part, tests)

def on_device(gradients, sign_words, sub_index, test_sketch):
    part = sketch_partial(gradients, sign_words, sub_index)
    return (scores_of(part, test_sketch) * (8192.0 ** -0.5)).reshape(1, 1024)

def solution(mesh):
    return jax.shard_map(on_device, mesh=mesh,
        in_specs=(P("ex", "feat"), P("feat"), P(), P("ex", None)),
        out_specs=P("ex", None), check_vma=False)
```

time: 79.1 us -> 60.3 us (0.76)
  between operations: 13.4 us -> 0.06 us
  waiting for transfers between devices: 3.57 us -> 0 us
  Pallas kernels: 56.8 us -> 55.2 us
    pallas_call x1, Pallas kernels: 43.2 us -> 27.9 us  [sketch_partial(): pl.pallas_call(kernel, out_shape=jax.ShapeDtypeStruct((8, 8, 128), jnp.fl...]
    pallas_call x1, Pallas kernels: 13.7 us -> 27.3 us  [scores_of(): pl.pallas_call(tail_kernel, out_shape=jax.ShapeDtypeStruct((8, 128), jnp....]
    all_gather x1 -> x0, waiting for transfers between devices: 3.56 us -> none  [on_device(): tests = lax.all_gather(cols, 'ex', axis=0, tiled=True)]
    unnamed x5 -> x0, local copies, waits for them, and re-layouts: 2.51 us -> none
    mul x0 -> x1, other arithmetic: none -> 1.27 us  [on_device(): return (scores_of(part, test_sketch) * 8192.0 ** (-0.5)).reshape(1, 1024)]
    add x0 -> x3, local copies, waits for them, and re-layouts: none -> 0.89 us  [sketch_partial(): kp = (c >> 10 & 1) * 128 + (c & 127)]
    shift_right_arithmetic x0 -> x3, local copies, waits for them, and re-layouts: none -> 0.89 us  [sketch_partial(): kq = c >> 11]
  transfers between devices with their start and end apart: 1 -> 0, of which waited for: 1 -> 0; matrix products, arithmetic and copies ran while one was open for 2% -> 0% of each run, Pallas kernels for 55% -> 0%
where the time goes in v3:
time: 60.3 us; the launch traced here: 60 us
  Pallas kernels  55.2 us (92%)
  local copies, waits for them, and re-layouts  2.67 us (4%)
  other arithmetic  2.05 us (3%)
    pallas_call x1, Pallas kernels, sketch_partial(): pl.pallas_call(kernel, out_shape=jax.ShapeDtypeStruct((8, 8, 128), jnp.fl...  27.9 us
    pallas_call x1, Pallas kernels, scores_of(): pl.pallas_call(tail_kernel, out_shape=jax.ShapeDtypeStruct((8, 128), jnp....  27.3 us
    mul x1, other arithmetic, on_device(): return (scores_of(part, test_sketch) * 8192.0 ** (-0.5)).reshape(1, 1024)  1.27 us

profile of v3, /device:TPU:1, one launch (start us, length us, event | category | flops | bytes accessed | tf_op | source)
XLA Modules:
  0.0 60.0 jit_solution(2257873556384134820)
XLA Ops:
  0.0 0.8 %shift-right-arithmetic_and_fusion = (s32[8192]{0:T(1024)S(1)}, s32[8192]{0:T(1024)S(1)}, s32[8192]{0:T(1024)S(1)}) fusion(s32[8192]{0:T(1024)} %param.9), kind=kLoop, calls=%fused_computation.1 | loop fusion | flops 73728 | bytes 131072 | tf_op jit(solution)/shard_map/and | solution.py:139
  0.8 0.1 reshape.96
  0.9 0.1 copy.10
  1.0 0.7 %and.85.ks_ref = s32[32,1,256]{2,1,0:T(1,128)} reshape(s32[32,8,32]{2,1,0:T(8,128)S(1)} %copy.10) | data formatting | bytes 65536 | tf_op jit(solution)/shard_map/and | solution.py:139
  1.7 0.1 reshape.99
  1.8 0.1 copy.8
  1.9 0.7 %reshape.94.kp_ref = s32[32,1,256]{2,1,0:T(1,128)} reshape(s32[32,8,32]{2,1,0:T(8,128)S(1)} %copy.8) | data formatting | bytes 65536 | tf_op jit(solution)/shard_map/add | solution.py:137
  2.6 0.1 shift_right_arithmetic.52
  2.7 0.1 copy.9
  2.8 0.7 %shift_right_arithmetic.54.kq_ref = s32[32,1,256]{2,1,0:T(1,128)} reshape(s32[32,8,32]{2,1,0:T(8,128)S(1)} %copy.9) | data formatting | bytes 65536 | tf_op jit(solution)/shard_map/shift_right_arithmetic | solution.py:138
  3.5 27.9 %shard_map.73.part_ref = f32[8,8,128]{2,1,0:T(8,128)} custom-call(bf16[32,4,1,65536]{3,2,1,0:T(2,128)(2,1)} %bitcast.9, s32[32,4,32,128]{3,2,1,0:T(8,128)} %bitcast.10, s32[32,1,256]{2,1,0:T(1,128)} %reshape.94.kp_ref, s32[32,1,256]{2,1,0:T(1,128)} %shift_right_arithmetic.54.kq_ref, s32[32,1,256]{2,1,0:T(1,128)} %and.85.ks_ref, ...), custom_call_target="tpu_custom_call" | custom-call | flops 16999999488 | bytes 37748736 | tf_op jit(solution)/shard_map/pallas_call | solution.py:147
  31.4 27.3 %shard_map.74 = f32[8,128]{1,0:T(8,128)} custom-call(f32[8,8,128]{2,1,0:T(8,128)} %shard_map.73.part_ref, bf16[64,8192]{1,0:T(8,128)(2,1)} %tests_ref.1), custom_call_target="tpu_custom_call" | custom-call | tf_op jit(solution)/shard_map/pallas_call | solution.py:242
  58.7 1.3 %broadcast_multiply_fusion = f32[8,128]{1,0:T(8,128)} fusion(f32[8,128]{1,0:T(8,128)} %shard_map.74), kind=kLoop, calls=%fused_computation.3 | loop fusion | flops 1024 | bytes 8192 | tf_op jit(solution)/shard_map/mul | solution.py:263

commit v4 on v3

v4 whole, which is shorter than its diff:
```python
import jax, jax.numpy as jnp, numpy as np
from jax import lax
from jax.experimental import pallas as pl
from jax.experimental.pallas import tpu as pltpu
from jax.sharding import PartitionSpec as P

def hada(n):
    h=np.ones((1,1))
    while h.shape[0]<n: h=np.block([[h,h],[h,-h]])
    return h

def k1_matrix():
    h32, h8 = hada(32), hada(8)
    rows = np.zeros((256,256))
    for j in range(16):
        for t in range(16):
            h5 = j + 16*(t//8); s = t%8
            rows[:, 16*j+t] = np.kron(h32[:,h5], h8[:,s])
    return rows

FB = 8192
NBLK = 32
NS = 12
UNITS = 4
TUNROLL = 4

FEATS, EXS = 8, 16
MESH = pl.DeviceIdType.MESH

def kernel(g_ref, w_ref, kp_ref, kq_ref, ks_ref, h4_ref, hm_ref, hb_ref, t_ref, out_ref,
           raw, words, psel, sq, xs0, xs1, ts, tests, mine1, recv1, mine2, recv2, sem, wsem,
           tsem, send0, got0, send1, got1, send2, got2):
    feat = lax.axis_index("feat")
    ex = lax.axis_index("ex")
    fpeers = [lax.rem(feat + d, FEATS) for d in range(1, FEATS)]
    epeers = [lax.rem(ex + d, EXS) for d in range(1, EXS)]
    barrier = pltpu.get_barrier_semaphore()
    for p in fpeers:
        pl.semaphore_signal(barrier, inc=1, device_id={"feat": p}, device_id_type=MESH)
    for p in epeers:
        pl.semaphore_signal(barrier, inc=1, device_id={"ex": p}, device_id_type=MESH)
    def tcopy(g):
        return pltpu.make_async_copy(t_ref.at[:, pl.ds(pl.multiple_of(g*1024 + feat*128, 128), 128)],
            tests.at[ex, :, g*128:g*128+128], tsem.at[g])
    def remote(src, dst, send, got, axis, p):
        return pltpu.make_async_remote_copy(src_ref=src, dst_ref=dst, send_sem=send, recv_sem=got,
            device_id={axis: p}, device_id_type=MESH)
    def gcopy(b):
        return pltpu.make_async_copy(g_ref.at[:, b // 8, :, pl.ds(pl.multiple_of((b % 8)*FB, FB), FB)], raw.at[b % NS], sem.at[b % NS])
    def wcopy(h2):
        return pltpu.make_async_copy(w_ref.at[:, h2], words.at[h2], wsem.at[h2])
    wcopy(0).start()
    for b in range(NS):
        gcopy(b).start()
    for h2 in range(1, 4):
        wcopy(h2).start()
    for g in range(8):
        tcopy(g).start()
    rows = lax.broadcasted_iota(jnp.int32, (256,256), 0)
    urow = lax.broadcasted_iota(jnp.int32, (32,256), 0)
    @pl.loop(0, 32//TUNROLL)
    def _(tt):
        for dt in range(TUNROLL):
            t = tt*TUNROLL + dt
            onehot = jnp.where(rows == kp_ref[t], 1.0, 0.0).astype(jnp.bfloat16)
            psel[t] = jnp.dot(hb_ref[...], onehot, preferred_element_type=jnp.float32).astype(jnp.bfloat16)
            v = urow & kq_ref[t]
            v = v ^ (v >> 4)
            v = v ^ (v >> 2)
            v = v ^ (v >> 1)
            sq[t] = jnp.where((v & 1) == 1, -1.0, 1.0)
    lane = lax.broadcasted_iota(jnp.int32, (8,128), 1)
    sub = lax.broadcasted_iota(jnp.int32, (8,128), 0)
    base = sub*8 + lane//16
    bit_lo = jnp.left_shift(1, lane % 16)
    bit_hi = jnp.left_shift(1, lane % 16 + 16)

    def prep(b, xs):
        slot = b % NS
        h2 = b // 8
        r0 = (b % 8)*UNITS
        for u in range(UNITS):
            for j in range(16):
                wlo = words[h2, j, pl.ds(r0 + u, 1), :]
                whi = words[h2, j+16, pl.ds(r0 + u, 1), :]
                wp = jnp.broadcast_to(wlo | (whi << 16), (8,128))
                for gam in range(2):
                    y = jnp.take_along_axis(wp, base + gam*64, axis=1)
                    parts = []
                    for hh, bit in ((j, bit_lo), (j+16, bit_hi)):
                        x = raw[slot, hh, :, u*2048 + gam*1024:u*2048 + gam*1024+1024]
                        x = x.astype(jnp.float32).reshape(8,128)
                        parts.append(jnp.where((y & bit) != 0, x, -x))
                    xs[16*j:16*j+16, u*256+gam*128:u*256+gam*128+128] = jnp.concatenate(parts, axis=0).astype(jnp.bfloat16)

    def mix(b, xs):
        for pair in range(UNITS//2):
            outs = [jnp.dot(hm_ref[...], xs[:, (2*pair+uu)*256:(2*pair+uu)*256+256], preferred_element_type=jnp.float32) for uu in range(2)]
            r0 = pl.multiple_of(b*(UNITS*8) + pair*16, 16)
            for t in range(32):
                ts[t, pl.ds(r0, 16), :] = jnp.concatenate([outs[0][8*t:8*t+8], outs[1][8*t:8*t+8]], axis=0).astype(jnp.bfloat16)

    def arrive(b):
        @pl.when(b < NBLK)
        def _():
            gcopy(b).wait()
        @pl.when((b < NBLK) & (b % 8 == 0))
        def _():
            wcopy(b // 8).wait()
    def refill(b):
        @pl.when(b < NBLK)
        def _():
            gcopy(b).start()

    pl.semaphore_wait(barrier, FEATS + EXS - 2)
    for g in range(8):
        tcopy(g).wait()
    for d, p in enumerate(epeers):
        remote(tests.at[ex], tests.at[ex], send0.at[d], got0.at[ex], "ex", p).start()
    arrive(0)
    prep(0, xs0)
    refill(NS)
    @pl.loop(0, NBLK//2)
    def _(i):
        b = 2*i
        arrive(b + 1)
        prep(b + 1, xs1)
        mix(b, xs0)
        refill(b + 1 + NS)
        arrive(b + 2)
        prep(jnp.minimum(b + 2, NBLK - 1), xs0)
        mix(b + 1, xs1)
        refill(b + 2 + NS)

    sub256 = lax.broadcasted_iota(jnp.int32, (8,256), 0)
    spread = (sub % 4)*32 + lane % 32
    @pl.loop(0, 8)
    def _(i):
        part = lax.rem(feat + 1 + i, FEATS)
        chunk = jnp.zeros((8,128), jnp.float32)
        for a in range(4):
            t = part*4 + a
            u = jnp.dot(ts[t], psel[t], preferred_element_type=jnp.float32)
            accs = [jnp.zeros((8,256), jnp.float32) for _ in range(4)]
            for m in range(32):
                s = jnp.broadcast_to(sq[t, m:m+1, :], (8,256))
                for h2 in range(4):
                    accs[h2] = accs[h2] + u[h2*256+m*8:h2*256+m*8+8] * s
            total = jnp.zeros((8,256), jnp.float32)
            for h2 in range(4):
                total = total + accs[h2] * h4_ref[h2:h2+1, :]
            total = jnp.where(sub256 == ks_ref[t], total, 0.0)
            row = jnp.broadcast_to(jnp.sum(total, axis=0, keepdims=True), (8,256))
            row = jnp.where(sub < 4, row[:, :128], row[:, 128:])
            row = jnp.take_along_axis(row, spread, axis=1)
            chunk = jnp.where(lane // 32 == a, row, chunk)
        mine1[part] = chunk
        @pl.when(i < FEATS - 1)
        def _():
            remote(mine1.at[part], recv1.at[feat], send1.at[i], got1.at[feat], "feat", part).start()

    recv1[feat] = mine1[feat]
    for d, p in enumerate(epeers):
        remote(tests.at[p], tests.at[p], send0.at[d], got0.at[p], "ex", p).wait_recv()
    for d, p in enumerate(fpeers):
        remote(mine1.at[p], recv1.at[p], send1.at[d], got1.at[p], "feat", p).wait_recv()
    sk = jnp.zeros((8,128), jnp.float32)
    for f in range(FEATS):
        v = sub & f
        v = (v ^ (v >> 1) ^ (v >> 2)) & 1
        sk = sk + jnp.where(v == 1, -recv1[f], recv1[f])
    sk = sk * (float(67108864) ** -0.5)
    row = jnp.concatenate([sk[g:g+1] for g in range(8)], axis=1)
    lhs = jnp.broadcast_to(row, (16, 1024)).astype(jnp.bfloat16)
    res = lax.dot_general(lhs, tests[...].reshape(1024, 1024), (((1,), (1,)), ((), ())), preferred_element_type=jnp.float32)
    mine2[...] = res[0:1]
    for d, p in enumerate(fpeers):
        remote(mine2, recv2.at[feat], send2.at[d], got2.at[feat], "feat", p).start()
    recv2[feat] = res[0:1]
    for d, p in enumerate(fpeers):
        remote(mine2, recv2.at[p], send2.at[d], got2.at[p], "feat", p).wait_recv()
    total = recv2[0]
    for f in range(1, FEATS):
        total = total + recv2[f]
    out_ref[...] = total
    for d, p in enumerate(epeers):
        remote(tests.at[ex], tests.at[ex], send0.at[d], got0.at[ex], "ex", p).wait_send()
    for d, p in enumerate(fpeers):
        remote(mine1.at[p], recv1.at[feat], send1.at[d], got1.at[feat], "feat", p).wait_send()
        remote(mine2, recv2.at[feat], send2.at[d], got2.at[feat], "feat", p).wait_send()

def scores_of(gradients, sign_words, sub_index, test_sketch):
    g = gradients.reshape(32, 4, 1, 65536)
    w = sign_words.reshape(32, 4, 32, 128)
    c = sub_index.reshape(8, 32, 32).transpose(1,0,2).reshape(32,1,256) & 65535
    kp = ((c >> 10) & 1)*128 + (c & 127)
    kq = c >> 11
    ks = (c >> 7) & 7
    col = np.arange(256)
    hh2 = (col >> 3) & 3
    h4 = jnp.asarray(hada(4)[:, hh2], jnp.float32)
    hm = jnp.asarray(k1_matrix(), jnp.bfloat16)
    hb = jnp.asarray(hada(256), jnp.bfloat16)
    anyspec = pl.BlockSpec(memory_space=pl.ANY)
    vm = pl.BlockSpec(memory_space=pltpu.VMEM)
    dma = pltpu.SemaphoreType.DMA
    return pl.pallas_call(
        kernel,
        out_shape=jax.ShapeDtypeStruct((1,1024), jnp.float32),
        in_specs=[anyspec, anyspec, vm, vm, vm, vm, vm, vm, anyspec],
        out_specs=vm,
        scratch_shapes=[
            pltpu.VMEM((NS, 32, 1, FB), jnp.bfloat16),
            pltpu.VMEM((4, 32, 32, 128), jnp.int32),
            pltpu.VMEM((32, 256, 256), jnp.bfloat16),
            pltpu.VMEM((32, 32, 256), jnp.float32),
            pltpu.VMEM((256, UNITS*256), jnp.bfloat16),
            pltpu.VMEM((256, UNITS*256), jnp.bfloat16),
            pltpu.VMEM((32, 1024, 256), jnp.bfloat16),
            pltpu.VMEM((EXS, 64, 1024), jnp.bfloat16),
            pltpu.VMEM((FEATS, 8, 128), jnp.float32),
            pltpu.VMEM((FEATS, 8, 128), jnp.float32),
            pltpu.VMEM((1, 1024), jnp.float32),
            pltpu.VMEM((FEATS, 1, 1024), jnp.float32),
            dma((NS,)), dma((4,)), dma((8,)), dma((EXS - 1,)), dma((EXS,)),
            dma((FEATS - 1,)), dma((FEATS,)), dma((FEATS - 1,)), dma((FEATS,)),
        ],
        compiler_params=pltpu.CompilerParams(collective_id=0, has_side_effects=True, vmem_limit_bytes=60*1024*1024),
        cost_estimate=pl.CostEstimate(flops=17_000_000_000, bytes_accessed=36*1024*1024, transcendentals=0),
    )(g, w, kp, kq, ks, h4, hm, hb, test_sketch)

def on_device(gradients, sign_words, sub_index, test_sketch):
    return scores_of(gradients, sign_words, sub_index, test_sketch) * (8192.0 ** -0.5)

def solution(mesh):
    return jax.shard_map(on_device, mesh=mesh,
        in_specs=(P("ex", "feat"), P("feat"), P(), P("ex", None)),
        out_specs=P("ex", None), check_vma=False)
```

time: 60.3 us -> 52.2 us (0.87)
  Pallas kernels: 55.2 us -> 47.2 us
    pallas_call x2 -> x1, Pallas kernels: 55.2 us -> 47.2 us  [scores_of(): pl.pallas_call(kernel, out_shape=jax.ShapeDtypeStruct((1, 1024), jnp.floa...]
where the time goes in v4:
time: 52.2 us; the launch traced here: 52 us
  Pallas kernels  47.2 us (90%)
  local copies, waits for them, and re-layouts  2.68 us (5%)
  other arithmetic  2.05 us (4%)
    pallas_call x1, Pallas kernels, scores_of(): pl.pallas_call(kernel, out_shape=jax.ShapeDtypeStruct((1, 1024), jnp.floa...  47.2 us
    mul x1, other arithmetic, on_device(): scores_of(gradients, sign_words, sub_index, test_sketch) * 8192.0 ** (-0.5)  1.28 us

profile of v4, /device:TPU:1, one launch (start us, length us, event | category | flops | bytes accessed | tf_op | source)
XLA Modules:
  0.0 52.0 jit_solution(12574222562725270580)
XLA Ops:
  0.0 0.8 %shift-right-arithmetic_and_fusion = (s32[8192]{0:T(1024)S(1)}, s32[8192]{0:T(1024)S(1)}, s32[8192]{0:T(1024)S(1)}) fusion(s32[8192]{0:T(1024)} %param.9), kind=kLoop, calls=%fused_computation.1 | loop fusion | flops 73728 | bytes 131072 | tf_op jit(solution)/shard_map/and | solution.py:198
  0.8 0.1 reshape.92
  0.9 0.1 copy.10
  1.0 0.7 %and.85.ks_ref = s32[32,1,256]{2,1,0:T(1,128)} reshape(s32[32,8,32]{2,1,0:T(8,128)S(1)} %copy.10) | data formatting | bytes 65536 | tf_op jit(solution)/shard_map/and | solution.py:198
  1.7 0.1 reshape.95
  1.8 0.1 copy.8
  1.9 0.7 %reshape.90.kp_ref = s32[32,1,256]{2,1,0:T(1,128)} reshape(s32[32,8,32]{2,1,0:T(8,128)S(1)} %copy.8) | data formatting | bytes 65536 | tf_op jit(solution)/shard_map/add | solution.py:196
  2.6 0.1 shift_right_arithmetic.52
  2.7 0.1 copy.9
  2.8 0.7 %shift_right_arithmetic.54.kq_ref = s32[32,1,256]{2,1,0:T(1,128)} reshape(s32[32,8,32]{2,1,0:T(8,128)S(1)} %copy.9) | data formatting | bytes 65536 | tf_op jit(solution)/shard_map/shift_right_arithmetic | solution.py:197
  3.5 47.2 %shard_map.73 = f32[1,1024]{1,0:T(1,128)} custom-call(bf16[32,4,1,65536]{3,2,1,0:T(2,128)(2,1)} %bitcast.8, s32[32,4,32,128]{3,2,1,0:T(8,128)} %bitcast.9, s32[32,1,256]{2,1,0:T(1,128)} %reshape.90.kp_ref, s32[32,1,256]{2,1,0:T(1,128)} %shift_right_arithmetic.54.kq_ref, s32[32,1,256]{2,1,0:T(1,128)} %and.85.ks_ref, f32[4,256]{1,0:T(4,128)} %constant.22.clone.h4_ref, ...), custom_call_target="tpu_custom_call" | custom-call | flops 16999999488 | bytes 37748736 | tf_op jit(solution)/shard_map/pallas_call | solution.py:207
  50.7 1.3 %broadcast_multiply_fusion = f32[1,1024]{1,0:T(1,128)} fusion(f32[1,1024]{1,0:T(1,128)} %shard_map.73), kind=kLoop, calls=%fused_computation.3 | loop fusion | flops 1024 | bytes 8192 | tf_op jit(solution)/shard_map/mul | solution.py:233

commit v5 on v4

v5 whole, which is shorter than its diff:
```python
import jax, jax.numpy as jnp, numpy as np
from jax import lax
from jax.experimental import pallas as pl
from jax.experimental.pallas import tpu as pltpu
from jax.sharding import PartitionSpec as P

def hada(n):
    h=np.ones((1,1))
    while h.shape[0]<n: h=np.block([[h,h],[h,-h]])
    return h

def k1_matrix():
    h32, h8 = hada(32), hada(8)
    rows = np.zeros((256,256))
    for j in range(16):
        for t in range(16):
            h5 = j + 16*(t//8); s = t%8
            rows[:, 16*j+t] = np.kron(h32[:,h5], h8[:,s])
    return rows

FB = 8192
NBLK = 32
NS = 12
UNITS = 4
TUNROLL = 4

FEATS, EXS, XS = 8, 16, 4
MESH = pl.DeviceIdType.MESH

def kernel(g_ref, w_ref, kp_ref, kq_ref, ks_ref, h4_ref, hm_ref, hb_ref, t_ref, out_ref,
           raw, words, psel, sq, xs0, xs1, tsa, tsb, acc, tstage, tests, mine1, recv1, mine2, recv2, sem, wsem,
           tsem, send0, got0, send1, got1, send2, got2):
    feat = lax.axis_index("feat")
    ex = lax.axis_index("ex")
    xpos = lax.rem(ex, XS)
    zpos = ex // XS
    group = [(df, dx, lax.rem(feat + df, FEATS), lax.rem(xpos + dx, XS)) for df in range(FEATS) for dx in range(XS) if df or dx]
    epeers = [lax.rem(ex + d, EXS) for d in range(1, EXS)]
    far = [lax.rem(zpos + dz, EXS // XS)*XS + x for dz in range(1, EXS // XS) for x in range(XS)]
    me = feat*XS + xpos
    barrier = pltpu.get_barrier_semaphore()
    for _, _, f, x in group:
        pl.semaphore_signal(barrier, inc=1, device_id=(f, zpos*XS + x), device_id_type=MESH)
    for e in far:
        pl.semaphore_signal(barrier, inc=1, device_id=(feat, e), device_id_type=MESH)
    def tcopy(x, r):
        return pltpu.make_async_copy(t_ref.at[:, pl.ds(pl.multiple_of((2*x + r)*1024 + feat*128, 128), 128)],
            tstage.at[x, :, r*128:r*128+128], tsem.at[2*x + r])
    def remote(src, dst, send, got, f, e):
        return pltpu.make_async_remote_copy(src_ref=src, dst_ref=dst, send_sem=send, recv_sem=got,
            device_id=(f, e), device_id_type=MESH)
    def to_tests(d, e, slot):
        return remote(tstage.at[lax.rem(e, XS)], tests.at[slot], send0.at[d], got0.at[slot], feat, e)
    def to_share(i, dx, f, x, slot):
        return remote(mine1.at[f, x], recv1.at[slot], send1.at[i*XS + dx], got1.at[slot], f, zpos*XS + x)
    def to_score(df, dx, f, x, slot):
        return remote(mine2.at[x], recv2.at[slot], send2.at[df*XS + dx], got2.at[slot], f, zpos*XS + x)
    def gcopy(b):
        return pltpu.make_async_copy(g_ref.at[:, b // 8, :, pl.ds(pl.multiple_of((b % 8)*FB, FB), FB)], raw.at[b % NS], sem.at[b % NS])
    def wcopy(h2):
        return pltpu.make_async_copy(w_ref.at[:, h2], words.at[h2], wsem.at[h2])
    wcopy(0).start()
    for b in range(NS):
        gcopy(b).start()
    for h2 in range(1, 4):
        wcopy(h2).start()
    for x in range(XS):
        for r in range(2):
            tcopy(x, r).start()
    rows = lax.broadcasted_iota(jnp.int32, (256,256), 0)
    urow = lax.broadcasted_iota(jnp.int32, (32,256), 0)
    @pl.loop(0, 32//TUNROLL)
    def _(tt):
        for dt in range(TUNROLL):
            t = tt*TUNROLL + dt
            onehot = jnp.where(rows == kp_ref[t], 1.0, 0.0).astype(jnp.bfloat16)
            psel[t] = jnp.dot(hb_ref[...], onehot, preferred_element_type=jnp.float32).astype(jnp.bfloat16)
            v = urow & kq_ref[t]
            v = v ^ (v >> 4)
            v = v ^ (v >> 2)
            v = v ^ (v >> 1)
            sq[t] = jnp.where((v & 1) == 1, -1.0, 1.0)
    lane = lax.broadcasted_iota(jnp.int32, (8,128), 1)
    sub = lax.broadcasted_iota(jnp.int32, (8,128), 0)
    base = sub*8 + lane//16
    bit_lo = jnp.left_shift(1, lane % 16)
    bit_hi = jnp.left_shift(1, lane % 16 + 16)

    def prep(b, xs):
        slot = b % NS
        h2 = b // 8
        r0 = (b % 8)*UNITS
        for u in range(UNITS):
            for j in range(16):
                wlo = words[h2, j, pl.ds(r0 + u, 1), :]
                whi = words[h2, j+16, pl.ds(r0 + u, 1), :]
                wp = jnp.broadcast_to(wlo | (whi << 16), (8,128))
                for gam in range(2):
                    y = jnp.take_along_axis(wp, base + gam*64, axis=1)
                    parts = []
                    for hh, bit in ((j, bit_lo), (j+16, bit_hi)):
                        x = raw[slot, hh, :, u*2048 + gam*1024:u*2048 + gam*1024+1024]
                        x = x.astype(jnp.float32).reshape(8,128)
                        parts.append(jnp.where((y & bit) != 0, x, -x))
                    xs[2*u + gam, 16*j:16*j+16, :] = jnp.concatenate(parts, axis=0).astype(jnp.bfloat16)

    def mix(b, xs, ts):
        for pair in range(UNITS//2):
            outs = [jnp.dot(hm_ref[...], jnp.concatenate([xs[4*pair + 2*uu], xs[4*pair + 2*uu + 1]], axis=1), preferred_element_type=jnp.float32) for uu in range(2)]
            r0 = pl.multiple_of((b % 8)*(UNITS*8) + pair*16, 16)
            for t in range(32):
                for half in range(2):
                    c = half*128
                    ts[t, half, pl.ds(r0, 16), :] = jnp.concatenate([outs[0][8*t:8*t+8, c:c+128], outs[1][8*t:8*t+8, c:c+128]], axis=0).astype(jnp.bfloat16)

    def pick(h2, t, ts):
        u = jnp.dot(jnp.concatenate([ts[t, 0], ts[t, 1]], axis=1), psel[t], preferred_element_type=jnp.float32)
        tot = jnp.zeros((8,256), jnp.float32)
        for m in range(32):
            tot = tot + u[8*m:8*m+8] * jnp.broadcast_to(sq[t, m:m+1, :], (8,256))
        return tot * h4_ref[h2:h2+1, :]

    def arrive(b):
        @pl.when(b < NBLK)
        def _():
            gcopy(b).wait()
        @pl.when((b < NBLK) & (b % 8 == 0))
        def _():
            wcopy(b // 8).wait()
    def refill(b):
        @pl.when(b < NBLK)
        def _():
            gcopy(b).start()

    arrive(0)
    prep(0, xs0)
    refill(NS)
    for h2 in range(4):
        new, old = (tsa, tsb) if h2 % 2 == 0 else (tsb, tsa)
        @pl.loop(0, 4)
        def _(i):
            b = 8*h2 + 2*i
            if h2 == 0:
                @pl.when(i == 1)
                def _():
                    pl.semaphore_wait(barrier, len(group) + len(far))
                    for x in range(XS):
                        for r in range(2):
                            tcopy(x, r).wait()
                    for d, e in enumerate(epeers):
                        to_tests(d, e, ex).start()
            arrive(b + 1)
            arrive(b + 2)
            for k, (xa, xb) in enumerate(((xs1, xs0), (xs0, xs1))):
                prep(jnp.minimum(b + k + 1, NBLK - 1), xa)
                mix(b + k, xb, new)
                if h2 > 0:
                    for dt in range(4):
                        t = 8*i + 4*k + dt
                        val = pick(h2 - 1, t, old)
                        acc[t] = val if h2 == 1 else acc[t] + val
            refill(b + 1 + NS)
            refill(b + 2 + NS)

    sub256 = lax.broadcasted_iota(jnp.int32, (8,256), 0)
    spread = (sub % 4)*32 + lane % 32
    @pl.loop(0, 8)
    def _(i):
        part = lax.rem(feat + 1 + i, FEATS)
        chunk = jnp.zeros((8,128), jnp.float32)
        for a in range(4):
            t = part*4 + a
            total = acc[t] + pick(3, t, tsb)
            total = jnp.where(sub256 == ks_ref[t], total, 0.0)
            row = jnp.broadcast_to(jnp.sum(total, axis=0, keepdims=True), (8,256))
            row = jnp.where(sub < 4, row[:, :128], row[:, 128:])
            row = jnp.take_along_axis(row, spread, axis=1)
            chunk = jnp.where(lane // 32 == a, row, chunk)
        for x in range(XS):
            mine1[part, x] = chunk[2*x:2*x+2]
        for dx in range(XS):
            @pl.when((i < FEATS - 1) | (dx > 0))
            def _():
                to_share(i, dx, part, lax.rem(xpos + dx, XS), me).start()

    recv1[me] = mine1[feat, xpos]
    tests[ex] = tstage[xpos]
    for d, e in enumerate(epeers):
        to_tests(d, e, e).wait_recv()
    for df, dx, f, x in group:
        to_share((df + 7) % 8, dx, f, x, f*XS + x).wait_recv()
    entry = 2*xpos + lax.broadcasted_iota(jnp.int32, (2,128), 0)
    lines = []
    for x in range(XS):
        sk = jnp.zeros((2,128), jnp.float32)
        for f in range(FEATS):
            v = entry & f
            v = (v ^ (v >> 1) ^ (v >> 2)) & 1
            sk = sk + jnp.where(v == 1, -recv1[f*XS + x], recv1[f*XS + x])
        sk = sk * (float(67108864) ** -0.5)
        lines.append(jnp.concatenate([sk[0:1], sk[1:2]], axis=1))
    lhs = jnp.concatenate(lines*4, axis=0).astype(jnp.bfloat16)
    res = lax.dot_general(lhs, tests[...].reshape(1024, 256), (((1,), (1,)), ((), ())), preferred_element_type=jnp.float32)
    for x in range(XS):
        mine2[x] = res[x:x+1]
    for df, dx, f, x in group:
        to_score(df, dx, f, x, me).start()
    recv2[me] = mine2[xpos]
    for df, dx, f, x in group:
        to_score(df, dx, f, x, f*XS + x).wait_recv()
    total = recv2[0]
    for f in range(1, FEATS*XS):
        total = total + recv2[f]
    out_ref[...] = total
    for d, e in enumerate(epeers):
        to_tests(d, e, ex).wait_send()
    for df, dx, f, x in group:
        to_share((df + 7) % 8, dx, f, x, me).wait_send()
        to_score(df, dx, f, x, me).wait_send()

def scores_of(gradients, sign_words, sub_index, test_sketch):
    g = gradients.reshape(32, 4, 1, 65536)
    w = sign_words.reshape(32, 4, 32, 128)
    c = sub_index.reshape(8, 32, 32).transpose(1,0,2).reshape(32,1,256) & 65535
    kp = ((c >> 10) & 1)*128 + (c & 127)
    kq = c >> 11
    ks = (c >> 7) & 7
    col = np.arange(256)
    hh2 = (col >> 3) & 3
    h4 = jnp.asarray(hada(4)[:, hh2], jnp.float32)
    hm = jnp.asarray(k1_matrix(), jnp.bfloat16)
    hb = jnp.asarray(hada(256), jnp.bfloat16)
    anyspec = pl.BlockSpec(memory_space=pl.ANY)
    vm = pl.BlockSpec(memory_space=pltpu.VMEM)
    dma = pltpu.SemaphoreType.DMA
    return pl.pallas_call(
        kernel,
        out_shape=jax.ShapeDtypeStruct((1,1024), jnp.float32),
        in_specs=[anyspec, anyspec, vm, vm, vm, vm, vm, vm, anyspec],
        out_specs=vm,
        scratch_shapes=[
            pltpu.VMEM((NS, 32, 1, FB), jnp.bfloat16),
            pltpu.VMEM((4, 32, 32, 128), jnp.int32),
            pltpu.VMEM((32, 256, 256), jnp.bfloat16),
            pltpu.VMEM((32, 32, 256), jnp.float32),
            pltpu.VMEM((2*UNITS, 256, 128), jnp.bfloat16),
            pltpu.VMEM((2*UNITS, 256, 128), jnp.bfloat16),
            pltpu.VMEM((32, 2, 256, 128), jnp.bfloat16),
            pltpu.VMEM((32, 2, 256, 128), jnp.bfloat16),
            pltpu.VMEM((32, 8, 256), jnp.float32),
            pltpu.VMEM((XS, 64, 256), jnp.bfloat16),
            pltpu.VMEM((EXS, 64, 256), jnp.bfloat16),
            pltpu.VMEM((FEATS, XS, 2, 128), jnp.float32),
            pltpu.VMEM((FEATS*XS, 2, 128), jnp.float32),
            pltpu.VMEM((XS, 1, 1024), jnp.float32),
            pltpu.VMEM((FEATS*XS, 1, 1024), jnp.float32),
            dma((NS,)), dma((4,)), dma((8,)), dma((EXS - 1,)), dma((EXS,)),
            dma((FEATS*XS,)), dma((FEATS*XS,)), dma((FEATS*XS,)), dma((FEATS*XS,)),
        ],
        compiler_params=pltpu.CompilerParams(collective_id=0, has_side_effects=True, vmem_limit_bytes=60*1024*1024),
        cost_estimate=pl.CostEstimate(flops=17_000_000_000, bytes_accessed=36*1024*1024, transcendentals=0),
    )(g, w, kp, kq, ks, h4, hm, hb, test_sketch)

def on_device(gradients, sign_words, sub_index, test_sketch):
    return scores_of(gradients, sign_words, sub_index, test_sketch) * (8192.0 ** -0.5)

def solution(mesh):
    return jax.shard_map(on_device, mesh=mesh,
        in_specs=(P("ex", "feat"), P("feat"), P(), P("ex", None)),
        out_specs=P("ex", None), check_vma=False)
```

time: 52.2 us -> 46.1 us (0.88)
  Pallas kernels: 47.2 us -> 41.1 us
    pallas_call x1, Pallas kernels: 47.2 us -> 41.1 us  [scores_of(): pl.pallas_call(kernel, out_shape=jax.ShapeDtypeStruct((1, 1024), jnp.floa...]
where the time goes in v5:
time: 46.1 us; the launch traced here: 45.9 us
  Pallas kernels  41.1 us (89%)
  local copies, waits for them, and re-layouts  2.68 us (6%)
  other arithmetic  2.05 us (4%)
    pallas_call x1, Pallas kernels, scores_of(): pl.pallas_call(kernel, out_shape=jax.ShapeDtypeStruct((1, 1024), jnp.floa...  41.1 us
    mul x1, other arithmetic, on_device(): scores_of(gradients, sign_words, sub_index, test_sketch) * 8192.0 ** (-0.5)  1.28 us

profile of v5, /device:TPU:1, one launch (start us, length us, event | category | flops | bytes accessed | tf_op | source)
XLA Modules:
  0.0 45.9 jit_solution(9876075487534517414)
XLA Ops:
  0.0 0.8 %shift-right-arithmetic_and_fusion = (s32[8192]{0:T(1024)S(1)}, s32[8192]{0:T(1024)S(1)}, s32[8192]{0:T(1024)S(1)}) fusion(s32[8192]{0:T(1024)} %param.9), kind=kLoop, calls=%fused_computation.1 | loop fusion | flops 73728 | bytes 131072 | tf_op jit(solution)/shard_map/and | solution.py:227
  0.8 0.1 reshape.92
  0.9 0.1 copy.10
  1.0 0.7 %and.85.ks_ref = s32[32,1,256]{2,1,0:T(1,128)} reshape(s32[32,8,32]{2,1,0:T(8,128)S(1)} %copy.10) | data formatting | bytes 65536 | tf_op jit(solution)/shard_map/and | solution.py:227
  1.7 0.1 reshape.95
  1.8 0.1 copy.8
  1.9 0.7 %reshape.90.kp_ref = s32[32,1,256]{2,1,0:T(1,128)} reshape(s32[32,8,32]{2,1,0:T(8,128)S(1)} %copy.8) | data formatting | bytes 65536 | tf_op jit(solution)/shard_map/add | solution.py:225
  2.6 0.1 shift_right_arithmetic.52
  2.7 0.1 copy.9
  2.8 0.7 %shift_right_arithmetic.54.kq_ref = s32[32,1,256]{2,1,0:T(1,128)} reshape(s32[32,8,32]{2,1,0:T(8,128)S(1)} %copy.9) | data formatting | bytes 65536 | tf_op jit(solution)/shard_map/shift_right_arithmetic | solution.py:226
  3.5 41.1 %shard_map.73 = f32[1,1024]{1,0:T(1,128)} custom-call(bf16[32,4,1,65536]{3,2,1,0:T(2,128)(2,1)} %bitcast.8, s32[32,4,32,128]{3,2,1,0:T(8,128)} %bitcast.9, s32[32,1,256]{2,1,0:T(1,128)} %reshape.90.kp_ref, s32[32,1,256]{2,1,0:T(1,128)} %shift_right_arithmetic.54.kq_ref, s32[32,1,256]{2,1,0:T(1,128)} %and.85.ks_ref, f32[4,256]{1,0:T(4,128)} %constant.22.clone.h4_ref, ...), custom_call_target="tpu_custom_call" | custom-call | flops 16999999488 | bytes 37748736 | tf_op jit(solution)/shard_map/pallas_call | solution.py:236
  44.6 1.3 %broadcast_multiply_fusion = f32[1,1024]{1,0:T(1,128)} fusion(f32[1,1024]{1,0:T(1,128)} %shard_map.73), kind=kLoop, calls=%fused_computation.3 | loop fusion | flops 1024 | bytes 8192 | tf_op jit(solution)/shard_map/mul | solution.py:265

commit v6 on v5

--- a/solution.py
+++ b/solution.py
@@ -27,7 +27,7 @@
 FEATS, EXS, XS = 8, 16, 4
 MESH = pl.DeviceIdType.MESH
 
-def kernel(g_ref, w_ref, kp_ref, kq_ref, ks_ref, h4_ref, hm_ref, hb_ref, t_ref, out_ref,
+def kernel(g_ref, w_ref, c_ref, h4_ref, hm_ref, hb_ref, t_ref, out_ref,
            raw, words, psel, sq, xs0, xs1, tsa, tsb, acc, tstage, tests, mine1, recv1, mine2, recv2, sem, wsem,
            tsem, send0, got0, send1, got1, send2, got2):
     feat = lax.axis_index("feat")
@@ -73,9 +73,10 @@
     def _(tt):
         for dt in range(TUNROLL):
             t = tt*TUNROLL + dt
-            onehot = jnp.where(rows == kp_ref[t], 1.0, 0.0).astype(jnp.bfloat16)
+            col = c_ref[t]
+            onehot = jnp.where(rows == ((col >> 10) & 1)*128 + (col & 127), 1.0, 0.0).astype(jnp.bfloat16)
             psel[t] = jnp.dot(hb_ref[...], onehot, preferred_element_type=jnp.float32).astype(jnp.bfloat16)
-            v = urow & kq_ref[t]
+            v = urow & (col >> 11)
             v = v ^ (v >> 4)
             v = v ^ (v >> 2)
             v = v ^ (v >> 1)
@@ -141,7 +142,7 @@
         def _(i):
             b = 8*h2 + 2*i
             if h2 == 0:
-                @pl.when(i == 1)
+                @pl.when(i == 3)
                 def _():
                     pl.semaphore_wait(barrier, len(group) + len(far))
                     for x in range(XS):
@@ -171,7 +172,7 @@
         for a in range(4):
             t = part*4 + a
             total = acc[t] + pick(3, t, tsb)
-            total = jnp.where(sub256 == ks_ref[t], total, 0.0)
+            total = jnp.where(sub256 == ((c_ref[t] >> 7) & 7), total, 0.0)
             row = jnp.broadcast_to(jnp.sum(total, axis=0, keepdims=True), (8,256))
             row = jnp.where(sub < 4, row[:, :128], row[:, 128:])
             row = jnp.take_along_axis(row, spread, axis=1)
@@ -222,9 +223,6 @@
     g = gradients.reshape(32, 4, 1, 65536)
     w = sign_words.reshape(32, 4, 32, 128)
     c = sub_index.reshape(8, 32, 32).transpose(1,0,2).reshape(32,1,256) & 65535
-    kp = ((c >> 10) & 1)*128 + (c & 127)
-    kq = c >> 11
-    ks = (c >> 7) & 7
     col = np.arange(256)
     hh2 = (col >> 3) & 3
     h4 = jnp.asarray(hada(4)[:, hh2], jnp.float32)
@@ -236,7 +234,7 @@
     return pl.pallas_call(
         kernel,
         out_shape=jax.ShapeDtypeStruct((1,1024), jnp.float32),
-        in_specs=[anyspec, anyspec, vm, vm, vm, vm, vm, vm, anyspec],
+        in_specs=[anyspec, anyspec, vm, vm, vm, vm, anyspec],
         out_specs=vm,
         scratch_shapes=[
             pltpu.VMEM((NS, 32, 1, FB), jnp.bfloat16),
@@ -259,7 +257,7 @@
         ],
         compiler_params=pltpu.CompilerParams(collective_id=0, has_side_effects=True, vmem_limit_bytes=60*1024*1024),
         cost_estimate=pl.CostEstimate(flops=17_000_000_000, bytes_accessed=36*1024*1024, transcendentals=0),
-    )(g, w, kp, kq, ks, h4, hm, hb, test_sketch)
+    )(g, w, c, h4, hm, hb, test_sketch)
 
 def on_device(gradients, sign_words, sub_index, test_sketch):
     return scores_of(gradients, sign_words, sub_index, test_sketch) * (8192.0 ** -0.5)

time: 46.1 us -> 43.7 us (0.948)
  local copies, waits for them, and re-layouts: 2.68 us -> 0.88 us
  Pallas kernels: 41.1 us -> 40.6 us
    add x3 -> x0, local copies, waits for them, and re-layouts: 0.9 us -> none  [scores_of(): kp = (c >> 10 & 1) * 128 + (c & 127)]
    shift_right_arithmetic x3 -> x0, local copies, waits for them, and re-layouts: 0.89 us -> none  [scores_of(): kq = c >> 11]
    pallas_call x1, Pallas kernels: 41.1 us -> 40.6 us  [scores_of(): pl.pallas_call(kernel, out_shape=jax.ShapeDtypeStruct((1, 1024), jnp.floa...]
where the time goes in v6:
time: 43.7 us; the launch traced here: 43.5 us
  Pallas kernels  40.6 us (93%)
  other arithmetic  2.03 us (5%)
  local copies, waits for them, and re-layouts  0.88 us (2%)
    pallas_call x1, Pallas kernels, scores_of(): pl.pallas_call(kernel, out_shape=jax.ShapeDtypeStruct((1, 1024), jnp.floa...  40.6 us
    mul x1, other arithmetic, on_device(): scores_of(gradients, sign_words, sub_index, test_sketch) * 8192.0 ** (-0.5)  1.27 us
    and x3, local copies, waits for them, and re-layouts, scores_of(): sub_index.reshape(8, 32, 32).transpose(1, 0, 2).reshape(32, 1, 256) & 65535  0.88 us

profile of v6, /device:TPU:1, one launch (start us, length us, event | category | flops | bytes accessed | tf_op | source)
XLA Modules:
  0.0 43.5 jit_solution(9120193654017877037)
XLA Ops:
  0.0 0.8 %broadcast_and_fusion = s32[8192]{0:T(1024)S(1)} fusion(s32[8192]{0:T(1024)} %param.9), kind=kLoop, calls=%fused_computation | loop fusion | flops 8192 | bytes 65536 | tf_op jit(solution)/shard_map/and | solution.py:225
  0.8 0.1 and.14
  0.9 0.1 copy.8
  0.9 0.7 %and.16.c_ref = s32[32,1,256]{2,1,0:T(1,128)} reshape(s32[32,8,32]{2,1,0:T(8,128)S(1)} %copy.8) | data formatting | bytes 65536 | tf_op jit(solution)/shard_map/and | solution.py:225
  1.7 40.6 %shard_map.73 = f32[1,1024]{1,0:T(1,128)} custom-call(bf16[32,4,1,65536]{3,2,1,0:T(2,128)(2,1)} %bitcast.4, s32[32,4,32,128]{3,2,1,0:T(8,128)} %bitcast.5, s32[32,1,256]{2,1,0:T(1,128)} %and.16.c_ref, f32[4,256]{1,0:T(4,128)} %constant.10.clone.h4_ref, bf16[256,256]{1,0:T(8,128)(2,1)} %constant.11.clone.hm_ref, bf16[256,256]{1,0:T(8,128)(2,1)} %constant.12.clone.hb_ref, ...), custom_call_target="tpu_custom_call" | custom-call | flops 16999999488 | bytes 37748736 | tf_op jit(solution)/shard_map/pallas_call | solution.py:234
  42.2 1.3 %broadcast_multiply_fusion = f32[1,1024]{1,0:T(1,128)} fusion(f32[1,1024]{1,0:T(1,128)} %shard_map.73), kind=kLoop, calls=%fused_computation.1 | loop fusion | flops 1024 | bytes 8192 | tf_op jit(solution)/shard_map/mul | solution.py:263
